TPU v7x, 512 devices: a whole 4x4x16 slice. The times are simulated.
512 devices in a mesh: tile: 128 (over x, z, core), band: 4 (over y).
Axes of the slice: x: 4, y: 4, z: 16, core: 2. Of those that a mesh axis runs over, the one named last changes fastest.
Arguments:
- column_state: bfloat16 [16384, 512], P('tile'), may hold values from -6 to 6
- sunlit: int32 [16384], P('tile'), may hold values from 0 to 1, as said below
- flagged: int32 [16384], P('tile'), may hold values from 0 to 1, as said below
- cos_zenith: bfloat16 [16384], P('tile'), may hold values from 0.05 to 1
- surface_albedo: bfloat16 [16384], P('tile'), may hold values from 0.29882812 to 0.8984375
- first_weight: bfloat16 [4, 512, 1024], P('band'), may hold values from -0.25 to 0.25
- first_bias: bfloat16 [4, 1024], P('band'), may hold values from -3 to 3
- second_weight: bfloat16 [4, 1024, 256], P('band'), may hold values from -0.1875 to 0.1875
- second_bias: bfloat16 [4, 256], P('band'), may hold values from -3 to 3
- absorption: float32 [224, 128], P('band'), may hold values from 0.00015625 to 0.15625
- scatter_albedo: float32 [224], P('band'), may hold values from 0.85 to 0.995
- solar_weight: float32 [224], P('band'), may hold values from 0.004464286 to 0.04464286
Outputs:
- fluxes: float32 [16384, 256], P(('tile', 'band'))
Inputs may be any that keep to these rules, and one draw needn't show every extreme that they name: Exactly a quarter of the 16384 columns are flagged, and every one of the 128 columns of at least one tile is flagged. Every flagged column is sunlit.
All inputs are finite; a program needn't handle non-finite values.
Results may differ from a plain program's by a relative error of at most 0.0017.
The roundings to bfloat16 on the way count: a program that leaves them out, or rounds other values in their place, can miss the bound.
Values may be sent and summed in bfloat16 or wider, within the bound.
No kernel may reach another device: no remote copies, remote signals or barrier semaphores. Data moves between devices by JAX's collectives and lax.ppermute only.
A program may use at most 64 MiB of HBM per device.

v0:
```python
import math

import jax
import jax.numpy as jnp
from jax import lax
from jax.experimental import pallas as pl
from jax.experimental.pallas import tpu as pltpu
from jax.sharding import PartitionSpec as P

SWEEPS = 4
DIFFUSIVITY = 1.66
LOG2E = 1.0 / math.log(2.0)
SUBLANES = 8
UNROLL = 8


def gelu(values):
    return 0.5 * values * (1.0 + lax.erf(values * math.sqrt(0.5)))


def group_sum(values):
    rows, lanes = values.shape
    return jnp.sum(values.reshape(rows // SUBLANES, SUBLANES, lanes), axis=0)


def column_kernel(
    state_ref,
    sunlit_ref,
    flagged_ref,
    zenith_ref,
    albedo_ref,
    bias_one_ref,
    bias_two_ref,
    absorption_ref,
    scatter_ref,
    solar_ref,
    weight_one_hbm,
    weight_two_hbm,
    out_ref,
    weight_one,
    weight_two,
    humid,
    humid_slant,
    keep,
    lost,
    source,
    falling,
    total,
    weight_sems,
):
    copy_one = pltpu.make_async_copy(weight_one_hbm, weight_one, weight_sems.at[0])
    copy_two = pltpu.make_async_copy(weight_two_hbm, weight_two, weight_sems.at[1])
    copy_one.start()
    copy_two.start()

    groups, levels = absorption_ref.shape
    columns = state_ref.shape[0]

    lit = sunlit_ref[...].astype(jnp.float32)
    chosen = flagged_ref[...].astype(jnp.float32)
    zenith = zenith_ref[...].astype(jnp.float32)
    albedo = albedo_ref[...].astype(jnp.float32)

    moisture = state_ref[:, levels : 2 * levels].astype(jnp.float32)
    humidity = (1.0 + 0.5 * jnp.tanh(moisture)).T
    humid[...] = humidity
    humid_slant[...] = humidity * (1.0 / (DIFFUSIVITY * zenith))
    scaled = absorption_ref[...] * (-DIFFUSIVITY * LOG2E)

    half_omega = jnp.broadcast_to(0.5 * scatter_ref[...], (levels, groups)).T
    half_omega = jnp.broadcast_to(half_omega[:, :1], (groups, columns))
    solar = jnp.broadcast_to(solar_ref[...], (levels, groups)).T
    solar = jnp.broadcast_to(solar[:, :1], (groups, columns))

    def setup(block, carry):
        direct, down = carry
        first_level = block * UNROLL
        window = pltpu.roll(scaled, (levels - first_level) % levels, 1)
        for step in range(UNROLL):
            level = first_level + step
            extinction = jnp.broadcast_to(window[:, step : step + 1], (groups, columns))
            passed = jnp.exp2(extinction * humid[pl.ds(level, 1), :])
            beam = jnp.exp2(extinction * humid_slant[pl.ds(level, 1), :])
            below = direct * beam
            first = half_omega * (direct - below)
            keep[level] = passed
            lost[level] = half_omega - half_omega * passed
            source[level] = first
            falling[level] = down
            total[level] = group_sum(direct)
            down = passed * down + first
            direct = below
        return direct, down

    nothing = jnp.zeros((groups, columns), jnp.float32)
    direct, down = lax.fori_loop(
        0, levels // UNROLL, setup, (solar * (zenith * lit), nothing)
    )

    def descend(last):
        def body(block, up):
            for step in range(UNROLL):
                level = levels - 1 - (block * UNROLL + step)
                falls = falling[level]
                emitted = source[level]
                if not last:
                    source[level] = lost[level] * (falls + up)
                up = keep[level] * up + emitted
                total[level] += group_sum(falls - up)
            return up

        return body

    def ascend(block, down):
        for step in range(UNROLL):
            level = block * UNROLL + step
            falling[level] = down
            down = keep[level] * down + source[level]
        return down

    up = albedo * (direct + down)
    for sweep in range(SWEEPS):
        lax.fori_loop(0, levels // UNROLL, descend(False), up)
        down = lax.fori_loop(0, levels // UNROLL, ascend, nothing)
        up = albedo * down
    lax.fori_loop(0, levels // UNROLL, descend(True), up)

    exact = (jnp.sum(total[...], axis=1) * chosen).T

    copy_one.wait()
    hidden = jnp.dot(state_ref[...], weight_one[...], preferred_element_type=jnp.float32)
    hidden = gelu(hidden + bias_one_ref[...].astype(jnp.float32)).astype(jnp.bfloat16)
    copy_two.wait()
    guess = jnp.dot(hidden, weight_two[...], preferred_element_type=jnp.float32)
    guess = 0.25 * (guess + bias_two_ref[...].astype(jnp.float32))
    mask = jnp.broadcast_to((1.0 - chosen) * lit, (levels, columns)).T
    out_ref[:, :levels] = exact + mask * guess[:, :levels]
    out_ref[:, levels:] = guess[:, levels:]


def shards(
    column_state,
    sunlit,
    flagged,
    cos_zenith,
    surface_albedo,
    first_weight,
    first_bias,
    second_weight,
    second_bias,
    absorption,
    scatter_albedo,
    solar_weight,
):
    columns, features = column_state.shape
    groups, levels = absorption.shape
    hidden = first_weight.shape[2]
    outputs = second_weight.shape[2]
    bands = lax.axis_size("band")
    in_vmem = pl.BlockSpec(memory_space=pltpu.VMEM)
    in_place = pl.BlockSpec(memory_space=pl.ANY)
    by_level = pltpu.VMEM((levels, groups, columns), jnp.float32)
    terms = pl.pallas_call(
        column_kernel,
        out_shape=jax.ShapeDtypeStruct((columns, outputs), jnp.float32),
        in_specs=[in_vmem] * 10 + [in_place] * 2,
        out_specs=in_vmem,
        scratch_shapes=[
            pltpu.VMEM((features, hidden), jnp.bfloat16),
            pltpu.VMEM((hidden, outputs), jnp.bfloat16),
            pltpu.VMEM((levels, columns), jnp.float32),
            pltpu.VMEM((levels, columns), jnp.float32),
            by_level,
            by_level,
            by_level,
            by_level,
            pltpu.VMEM((levels, SUBLANES, columns), jnp.float32),
            pltpu.SemaphoreType.DMA((2,)),
        ],
        compiler_params=pltpu.CompilerParams(vmem_limit_bytes=48 * 1024 * 1024),
        name="column_terms",
    )(
        column_state,
        sunlit.reshape(1, columns),
        flagged.reshape(1, columns),
        cos_zenith.reshape(1, columns),
        surface_albedo.reshape(1, columns),
        first_bias,
        second_bias,
        absorption,
        scatter_albedo.reshape(1, groups),
        solar_weight.reshape(1, groups),
        first_weight[0],
        second_weight[0],
    )
    blocks = lax.all_to_all(
        terms.reshape(bands, columns // bands, outputs), "band", split_axis=0, concat_axis=0, tiled=True
    )
    return jnp.sum(blocks, axis=0)


def solution(mesh):
    in_specs = (
        P("tile", None),
        P("tile"),
        P("tile"),
        P("tile"),
        P("tile"),
        P("band", None, None),
        P("band", None),
        P("band", None, None),
        P("band", None),
        P("band", None),
        P("band"),
        P("band"),
    )
    out_specs = P(("tile", "band"), None)
    return jax.shard_map(shards, mesh=mesh, in_specs=in_specs, out_specs=out_specs, check_vma=False)
```

profile of v0, /device:TPU:8, one launch (start us, length us, event | category | flops | bytes accessed | tf_op | source)
XLA Modules:
  0.0 29.6 jit_solution(13942473568306172658)
XLA Ops:
  0.0 0.0 copy-start.11
  0.0 0.0 copy-start.4
  0.0 0.0 copy-start.7
  0.0 0.0 copy-start.8
  0.0 0.0 copy-start.9
  0.0 0.0 copy-start.10
  0.0 0.0 copy-start.5
  0.0 0.0 copy-start.6
  0.1 0.6 %copy-done.11 = f32[56]{0:T(128)S(1)} copy-done((f32[56]{0:T(128)S(1)}, f32[56]{0:T(128)}, u32[]{:S(2)}) %copy-start.11) | copy-done | bytes 248
  0.7 0.0 copy-done.4
  0.7 0.0 copy-done.7
  0.7 0.0 copy-done.8
  0.7 0.0 copy-done.9
  0.7 0.0 copy-done.10
  0.7 0.0 copy-done.5
  0.8 0.0 copy-done.6
  0.8 0.0 copy-start
  0.8 1.2 %copy-done = bf16[1,512,1024]{2,1,0:T(8,128)(2,1)S(1)} copy-done((bf16[1,512,1024]{2,1,0:T(8,128)(2,1)S(1)}, bf16[1,512,1024]{2,1,0:T(8,128)(2,1)}, u32[]{:S(2)}) %copy-start) | copy-done | bytes 1048600
  2.0 0.0 copy-start.1
  2.0 1.0 %copy-done.1 = bf16[1,1024,256]{2,1,0:T(8,128)(2,1)S(1)} copy-done((bf16[1,1024,256]{2,1,0:T(8,128)(2,1)S(1)}, bf16[1,1024,256]{2,1,0:T(8,128)(2,1)}, u32[]{:S(2)}) %copy-start.1) | copy-done | bytes 524312
  3.0 0.0 copy-start.2
  3.0 0.9 %copy-done.2 = bf16[128,512]{1,0:T(8,128)(2,1)S(1)} copy-done((bf16[128,512]{1,0:T(8,128)(2,1)S(1)}, bf16[128,512]{1,0:T(8,128)(2,1)}, u32[]{:S(2)}) %copy-start.2) | copy-done | bytes 131096
  4.0 0.0 copy-start.3
  4.0 0.7 %copy-done.3 = f32[56,128]{1,0:T(8,128)S(1)} copy-done((f32[56,128]{1,0:T(8,128)S(1)}, f32[56,128]{1,0:T(8,128)}, u32[]{:S(2)}) %copy-start.3) | copy-done | bytes 28696
  4.7 11.6 %column_terms.1 = f32[128,256]{1,0:T(8,128)S(1)} custom-call(bf16[128,512]{1,0:T(8,128)(2,1)S(1)} %copy-done.2, s32[1,128]{1,0:T(1,128)S(1)} %bitcast.12, s32[1,128]{1,0:T(1,128)S(1)} %bitcast.13, bf16[1,128]{1,0:T(2,128)(2,1)S(1)} %bitcast.14, bf16[1,128]{1,0:T(2,128)(2,1)S(1)} %bitcast.15, bf16[1,1024]{1,0:T(2,128)(2,1)S(1)} %copy-done.4, ...), custom_call_target="tpu_custom_call" | custom-call | tf_op jit(solution)/shard_map/column_terms/pallas_call | solution.py:163
  16.3 12.7 %all_to_all.5 = f32[4,32,256]{2,1,0:T(8,128)S(1)} all-to-all(f32[4,32,256]{2,1,0:T(8,128)S(1)} %bitcast.10), channel_id=1, replica_groups=mesh['tile'=128,'band'=4] {'band'}, dimensions={0} | all-to-all | bytes 262144 | tf_op jit(solution)/shard_map/all_to_all | solution.py:196
  29.0 0.6 %reduce_sum.9 = f32[32,256]{1,0:T(8,128)} reduce(f32[4,32,256]{2,1,0:T(8,128)S(1)} %all_to_all.5, f32[]{:T(128)} %constant.0.clone.1), dimensions={0}, to_apply=%region_0.0 | reduce | flops 24576 | bytes 163844 | tf_op jit(solution)/shard_map/reduce_sum | solution.py:199
Async XLA Ops:
  0.0 0.7 %copy-start.11 = (f32[56]{0:T(128)S(1)}, f32[56]{0:T(128)}, u32[]{:S(2)}) copy-start(f32[56]{0:T(128)} %param.23) | copy-start | bytes 676
  0.0 0.7 %copy-start.4 = (bf16[1,1024]{1,0:T(2,128)(2,1)S(1)}, bf16[1,1024]{1,0:T(2,128)(2,1)}, u32[]{:S(2)}) copy-start(bf16[1,1024]{1,0:T(2,128)(2,1)} %bias_one_ref.1) | copy-start | bytes 6148
  0.0 0.7 %copy-start.7 = (s32[128]{0:T(128)S(1)}, s32[128]{0:T(128)}, u32[]{:S(2)}) copy-start(s32[128]{0:T(128)} %param.14) | copy-start | bytes 1540
  0.0 0.7 %copy-start.8 = (bf16[128]{0:T(256)(128)(2,1)S(1)}, bf16[128]{0:T(256)(128)(2,1)}, u32[]{:S(2)}) copy-start(bf16[128]{0:T(256)(128)(2,1)} %param.15) | copy-start | bytes 772
  0.0 0.7 %copy-start.9 = (bf16[128]{0:T(256)(128)(2,1)S(1)}, bf16[128]{0:T(256)(128)(2,1)}, u32[]{:S(2)}) copy-start(bf16[128]{0:T(256)(128)(2,1)} %param.16) | copy-start | bytes 772
  0.0 0.7 %copy-start.10 = (f32[56]{0:T(128)S(1)}, f32[56]{0:T(128)}, u32[]{:S(2)}) copy-start(f32[56]{0:T(128)} %param.22) | copy-start | bytes 676
  0.0 0.7 %copy-start.5 = (bf16[1,256]{1,0:T(2,128)(2,1)S(1)}, bf16[1,256]{1,0:T(2,128)(2,1)}, u32[]{:S(2)}) copy-start(bf16[1,256]{1,0:T(2,128)(2,1)} %bias_two_ref.1) | copy-start | bytes 1540
  0.0 0.7 %copy-start.6 = (s32[128]{0:T(128)S(1)}, s32[128]{0:T(128)}, u32[]{:S(2)}) copy-start(s32[128]{0:T(128)} %param.13) | copy-start | bytes 1540
  0.8 1.2 %copy-start = (bf16[1,512,1024]{2,1,0:T(8,128)(2,1)S(1)}, bf16[1,512,1024]{2,1,0:T(8,128)(2,1)}, u32[]{:S(2)}) copy-start(bf16[1,512,1024]{2,1,0:T(8,128)(2,1)} %param.17) | copy-start | bytes 3145732
  2.0 1.0 %copy-start.1 = (bf16[1,1024,256]{2,1,0:T(8,128)(2,1)S(1)}, bf16[1,1024,256]{2,1,0:T(8,128)(2,1)}, u32[]{:S(2)}) copy-start(bf16[1,1024,256]{2,1,0:T(8,128)(2,1)} %param.19) | copy-start | bytes 1572868
  3.0 0.9 %copy-start.2 = (bf16[128,512]{1,0:T(8,128)(2,1)S(1)}, bf16[128,512]{1,0:T(8,128)(2,1)}, u32[]{:S(2)}) copy-start(bf16[128,512]{1,0:T(8,128)(2,1)} %state_ref.1) | copy-start | bytes 393220
  4.0 0.7 %copy-start.3 = (f32[56,128]{1,0:T(8,128)S(1)}, f32[56,128]{1,0:T(8,128)}, u32[]{:S(2)}) copy-start(f32[56,128]{1,0:T(8,128)} %absorption_ref.1) | copy-start | bytes 86020
where the time goes:
time: 30 us; the launch traced here: 29.6 us
  blocking collectives  12.7 us (42%)
  Pallas kernels  11.6 us (39%)
  local copies, waits for them, and re-layouts  4.65 us (16%)
  other arithmetic  0.62 us (2%)
    all_to_all x1, blocking collectives, shards(): lax.all_to_all(terms.reshape(bands, columns // bands, outputs), 'band', s...  12.7 us
    pallas_call x1, Pallas kernels, shards(): pl.pallas_call(column_kernel, out_shape=jax.ShapeDtypeStruct((columns, ou...  11.6 us
    unnamed x24, local copies, waits for them, and re-layouts  4.65 us
    reduce_sum x1, other arithmetic, shards(): return jnp.sum(blocks, axis=0)  0.62 us

commit v1 on v0

v1 whole, which is shorter than its diff:
```python
import math

import jax
import jax.numpy as jnp
from jax import lax
from jax.experimental import pallas as pl
from jax.experimental.pallas import tpu as pltpu
from jax.sharding import PartitionSpec as P

SWEEPS = 4
DIFFUSIVITY = 1.66
LOG2E = 1.0 / math.log(2.0)
SUBLANES = 8
DESCENT = 32


def gelu(values):
    return 0.5 * values * (1.0 + lax.erf(values * math.sqrt(0.5)))


def group_sum(values):
    return jnp.sum(values, axis=0)


def column_kernel(*refs):
    hbm, out_ref, local, (humid, humid_slant, keep, lost, source, falling, total, sems) = (
        refs[:12],
        refs[12],
        refs[13:25],
        refs[25:],
    )
    copies = [pltpu.make_async_copy(a, b, sems.at[i]) for i, (a, b) in enumerate(zip(hbm, local))]
    for copy in copies:
        copy.start()
    (
        state_ref,
        sunlit_ref,
        flagged_ref,
        zenith_ref,
        albedo_ref,
        bias_one_ref,
        bias_two_ref,
        absorption_ref,
        scatter_ref,
        solar_ref,
        weight_one_ref,
        weight_two_ref,
    ) = local
    for copy in copies[:10]:
        copy.wait()

    groups, levels = absorption_ref.shape
    columns = state_ref.shape[0]

    chains = groups // SUBLANES
    wide = (chains, SUBLANES, columns)

    def rows(level):
        return pl.ds(level * chains, chains)

    lit = sunlit_ref[...].astype(jnp.float32)
    chosen = flagged_ref[...].astype(jnp.float32)
    zenith = zenith_ref[...].astype(jnp.float32)
    albedo = albedo_ref[...].astype(jnp.float32)

    moisture = state_ref[:, levels : 2 * levels].astype(jnp.float32)
    humidity = (1.0 + 0.5 * jnp.tanh(moisture)).T
    humid[...] = humidity
    humid_slant[...] = humidity * (1.0 / (DIFFUSIVITY * zenith))
    scaled = absorption_ref[...] * (-DIFFUSIVITY * LOG2E)

    half_omega = jnp.broadcast_to(0.5 * scatter_ref[...], (levels, groups)).T
    half_omega = jnp.broadcast_to(half_omega[:, :1], (groups, columns)).reshape(wide)
    solar = jnp.broadcast_to(solar_ref[...], (levels, groups)).T
    solar = jnp.broadcast_to(solar[:, :1], (groups, columns)).reshape(wide)

    nothing = jnp.zeros(wide, jnp.float32)
    direct = solar * (zenith * lit)
    down = nothing
    for level in range(levels):
        extinction = jnp.broadcast_to(scaled[:, level : level + 1], (groups, columns)).reshape(wide)
        passed = jnp.exp2(extinction * humid[pl.ds(level, 1), :])
        beam = jnp.exp2(extinction * humid_slant[pl.ds(level, 1), :])
        below = direct * beam
        first = half_omega * (direct - below)
        keep[rows(level)] = passed
        lost[rows(level)] = half_omega - half_omega * passed
        source[rows(level)] = first
        falling[rows(level)] = down
        total[level] = group_sum(direct)
        down = passed * down + first
        direct = below

    def descend(last):
        def body(block, up):
            for step in range(DESCENT):
                level = levels - 1 - (block * DESCENT + step)
                falls = falling[rows(level)]
                emitted = source[rows(level)]
                if not last:
                    source[rows(level)] = lost[rows(level)] * (falls + up)
                up = keep[rows(level)] * up + emitted
                total[level] += group_sum(falls - up)
            return up

        return body

    def ascend():
        down = nothing
        for level in range(levels):
            falling[rows(level)] = down
            down = keep[rows(level)] * down + source[rows(level)]
        return down

    up = albedo * (direct + down)
    for sweep in range(SWEEPS):
        lax.fori_loop(0, levels // DESCENT, descend(False), up)
        up = albedo * ascend()
    lax.fori_loop(0, levels // DESCENT, descend(True), up)

    exact = (jnp.sum(total[...], axis=1) * chosen).T

    copies[10].wait()
    hidden = jnp.dot(state_ref[...], weight_one_ref[...], preferred_element_type=jnp.float32)
    hidden = gelu(hidden + bias_one_ref[...].astype(jnp.float32)).astype(jnp.bfloat16)
    copies[11].wait()
    guess = jnp.dot(hidden, weight_two_ref[...], preferred_element_type=jnp.float32)
    guess = 0.25 * (guess + bias_two_ref[...].astype(jnp.float32))
    mask = jnp.broadcast_to((1.0 - chosen) * lit, (levels, columns)).T
    out_ref[:, :levels] = exact + mask * guess[:, :levels]
    out_ref[:, levels:] = guess[:, levels:]


def shards(
    column_state,
    sunlit,
    flagged,
    cos_zenith,
    surface_albedo,
    first_weight,
    first_bias,
    second_weight,
    second_bias,
    absorption,
    scatter_albedo,
    solar_weight,
):
    columns, features = column_state.shape
    groups, levels = absorption.shape
    hidden = first_weight.shape[2]
    outputs = second_weight.shape[2]
    bands = lax.axis_size("band")
    operands = (
        column_state,
        sunlit.reshape(1, columns),
        flagged.reshape(1, columns),
        cos_zenith.reshape(1, columns),
        surface_albedo.reshape(1, columns),
        first_bias,
        second_bias,
        absorption,
        scatter_albedo.reshape(1, groups),
        solar_weight.reshape(1, groups),
        first_weight[0],
        second_weight[0],
    )
    chain_rows = levels * groups // SUBLANES
    terms = pl.pallas_call(
        column_kernel,
        out_shape=jax.ShapeDtypeStruct((columns, outputs), jnp.float32),
        in_specs=[pl.BlockSpec(memory_space=pltpu.HBM)] * len(operands),
        out_specs=pl.BlockSpec(memory_space=pltpu.VMEM),
        scratch_shapes=[pltpu.VMEM(x.shape, x.dtype) for x in operands]
        + [pltpu.VMEM((levels, columns), jnp.float32)] * 2
        + [pltpu.VMEM((chain_rows, SUBLANES, columns), jnp.float32)] * 4
        + [pltpu.VMEM((levels, SUBLANES, columns), jnp.float32)]
        + [pltpu.SemaphoreType.DMA((len(operands),))],
        compiler_params=pltpu.CompilerParams(vmem_limit_bytes=48 * 1024 * 1024),
        name="column_terms",
    )(*[pltpu.with_memory_space_constraint(x, pltpu.HBM) for x in operands])
    blocks = lax.all_to_all(
        terms.reshape(bands, columns // bands, outputs), "band", split_axis=0, concat_axis=0, tiled=True
    )
    return jnp.sum(blocks, axis=0)


def solution(mesh):
    in_specs = (
        P("tile", None),
        P("tile"),
        P("tile"),
        P("tile"),
        P("tile"),
        P("band", None, None),
        P("band", None),
        P("band", None, None),
        P("band", None),
        P("band", None),
        P("band"),
        P("band"),
    )
    out_specs = P(("tile", "band"), None)
    return jax.shard_map(shards, mesh=mesh, in_specs=in_specs, out_specs=out_specs, check_vma=False)
```

time: 30 us -> 23 us (0.77)
  local copies, waits for them, and re-layouts: 4.65 us -> 0 us
  Pallas kernels: 11.6 us -> 9.46 us
    unnamed x24 -> x0, local copies, waits for them, and re-layouts: 4.65 us -> none
    pallas_call x1, Pallas kernels: 11.6 us -> 9.46 us  [shards(): pl.pallas_call(column_kernel, out_shape=jax.ShapeDtypeStruct((columns, ou...]
where the time goes in v1:
time: 23 us; the launch traced here: 22.8 us
  blocking collectives  12.7 us (55%)
  Pallas kernels  9.46 us (41%)
  other arithmetic  0.62 us (3%)
    all_to_all x1, blocking collectives, shards(): lax.all_to_all(terms.reshape(bands, columns // bands, outputs), 'band', s...  12.7 us
    pallas_call x1, Pallas kernels, shards(): pl.pallas_call(column_kernel, out_shape=jax.ShapeDtypeStruct((columns, ou...  9.46 us
    reduce_sum x1, other arithmetic, shards(): return jnp.sum(blocks, axis=0)  0.62 us

profile of v1, /device:TPU:8, one launch (start us, length us, event | category | flops | bytes accessed | tf_op | source)
XLA Modules:
  0.0 22.8 jit_solution(1350109608316662429)
XLA Ops:
  0.0 9.5 %column_terms.1 = f32[128,256]{1,0:T(8,128)S(1)} custom-call(bf16[128,512]{1,0:T(8,128)(2,1)} %refs_0_.1, s32[1,128]{1,0:T(1,128)} %bitcast.12, s32[1,128]{1,0:T(1,128)} %bitcast.13, bf16[1,128]{1,0:T(2,128)(2,1)} %bitcast.14, bf16[1,128]{1,0:T(2,128)(2,1)} %bitcast.15, bf16[1,1024]{1,0:T(2,128)(2,1)} %refs_5_.1, bf16[1,256]{1,0:T(2,128)(2,1)} %refs_6_.1, ...), custom_call_target="tpu_custom_call" | custom-call | tf_op jit(solution)/shard_map/column_terms/pallas_call | solution.py:168
  9.5 12.7 %all_to_all.5 = f32[4,32,256]{2,1,0:T(8,128)S(1)} all-to-all(f32[4,32,256]{2,1,0:T(8,128)S(1)} %bitcast.9), channel_id=1, replica_groups=mesh['tile'=128,'band'=4] {'band'}, dimensions={0} | all-to-all | bytes 262144 | tf_op jit(solution)/shard_map/all_to_all | solution.py:181
  22.2 0.6 %reduce_sum.9 = f32[32,256]{1,0:T(8,128)} reduce(f32[4,32,256]{2,1,0:T(8,128)S(1)} %all_to_all.5, f32[]{:T(128)} %constant.0.clone.1), dimensions={0}, to_apply=%region_0.0 | reduce | flops 24576 | bytes 163844 | tf_op jit(solution)/shard_map/reduce_sum | solution.py:184

commit v2 on v1

--- a/solution.py
+++ b/solution.py
@@ -11,7 +11,6 @@
 DIFFUSIVITY = 1.66
 LOG2E = 1.0 / math.log(2.0)
 SUBLANES = 8
-DESCENT = 32
 
 
 def gelu(values):
@@ -30,7 +29,7 @@
         refs[25:],
     )
     copies = [pltpu.make_async_copy(a, b, sems.at[i]) for i, (a, b) in enumerate(zip(hbm, local))]
-    for copy in copies:
+    for copy in copies[:10]:
         copy.start()
     (
         state_ref,
@@ -48,6 +47,8 @@
     ) = local
     for copy in copies[:10]:
         copy.wait()
+    for copy in copies[10:]:
+        copy.start()
 
     groups, levels = absorption_ref.shape
     columns = state_ref.shape[0]
@@ -91,19 +92,18 @@
         down = passed * down + first
         direct = below
 
-    def descend(last):
-        def body(block, up):
-            for step in range(DESCENT):
-                level = levels - 1 - (block * DESCENT + step)
-                falls = falling[rows(level)]
-                emitted = source[rows(level)]
-                if not last:
-                    source[rows(level)] = lost[rows(level)] * (falls + up)
-                up = keep[rows(level)] * up + emitted
-                total[level] += group_sum(falls - up)
-            return up
-
-        return body
+    def descend(up, last):
+        for level in reversed(range(levels)):
+            falls = falling[rows(level)]
+            emitted = source[rows(level)]
+            if not last:
+                source[rows(level)] = lost[rows(level)] * (falls + up)
+            up = keep[rows(level)] * up + emitted
+            net = total[level] + group_sum(falls - up)
+            if last:
+                humid[pl.ds(level, 1), :] = jnp.sum(net, axis=0, keepdims=True)
+            else:
+                total[level] = net
 
     def ascend():
         down = nothing
@@ -112,18 +112,19 @@
             down = keep[rows(level)] * down + source[rows(level)]
         return down
 
-    up = albedo * (direct + down)
-    for sweep in range(SWEEPS):
-        lax.fori_loop(0, levels // DESCENT, descend(False), up)
-        up = albedo * ascend()
-    lax.fori_loop(0, levels // DESCENT, descend(True), up)
-
-    exact = (jnp.sum(total[...], axis=1) * chosen).T
-
-    copies[10].wait()
+    def sweep(_, up):
+        descend(up, False)
+        return albedo * ascend()
+
+    up = lax.fori_loop(0, SWEEPS, sweep, albedo * (direct + down))
+    for copy in copies[10:]:
+        copy.wait()
+    descend(up, True)
+
+    exact = (humid[...] * chosen).T
+
     hidden = jnp.dot(state_ref[...], weight_one_ref[...], preferred_element_type=jnp.float32)
     hidden = gelu(hidden + bias_one_ref[...].astype(jnp.float32)).astype(jnp.bfloat16)
-    copies[11].wait()
     guess = jnp.dot(hidden, weight_two_ref[...], preferred_element_type=jnp.float32)
     guess = 0.25 * (guess + bias_two_ref[...].astype(jnp.float32))
     mask = jnp.broadcast_to((1.0 - chosen) * lit, (levels, columns)).T

time: 23 us -> 21.8 us (0.948)
  Pallas kernels: 9.46 us -> 8.29 us
    pallas_call x1, Pallas kernels: 9.46 us -> 8.29 us  [shards(): pl.pallas_call(column_kernel, out_shape=jax.ShapeDtypeStruct((columns, ou...]
where the time goes in v2:
time: 21.8 us; the launch traced here: 21.6 us
  blocking collectives  12.7 us (58%)
  Pallas kernels  8.29 us (38%)
  other arithmetic  0.62 us (3%)
    all_to_all x1, blocking collectives, shards(): lax.all_to_all(terms.reshape(bands, columns // bands, outputs), 'band', s...  12.7 us
    pallas_call x1, Pallas kernels, shards(): pl.pallas_call(column_kernel, out_shape=jax.ShapeDtypeStruct((columns, ou...  8.29 us
    reduce_sum x1, other arithmetic, shards(): return jnp.sum(blocks, axis=0)  0.62 us

profile of v2, /device:TPU:8, one launch (start us, length us, event | category | flops | bytes accessed | tf_op | source)
XLA Modules:
  0.0 21.6 jit_solution(7561486644128304925)
XLA Ops:
  0.0 8.3 %column_terms.1 = f32[128,256]{1,0:T(8,128)S(1)} custom-call(bf16[128,512]{1,0:T(8,128)(2,1)} %refs_0_.1, s32[1,128]{1,0:T(1,128)} %bitcast.12, s32[1,128]{1,0:T(1,128)} %bitcast.13, bf16[1,128]{1,0:T(2,128)(2,1)} %bitcast.14, bf16[1,128]{1,0:T(2,128)(2,1)} %bitcast.15, bf16[1,1024]{1,0:T(2,128)(2,1)} %refs_5_.1, bf16[1,256]{1,0:T(2,128)(2,1)} %refs_6_.1, ...), custom_call_target="tpu_custom_call" | custom-call | tf_op jit(solution)/shard_map/column_terms/pallas_call | solution.py:169
  8.3 12.7 %all_to_all.5 = f32[4,32,256]{2,1,0:T(8,128)S(1)} all-to-all(f32[4,32,256]{2,1,0:T(8,128)S(1)} %bitcast.9), channel_id=1, replica_groups=mesh['tile'=128,'band'=4] {'band'}, dimensions={0} | all-to-all | bytes 262144 | tf_op jit(solution)/shard_map/all_to_all | solution.py:182
  21.0 0.6 %reduce_sum.9 = f32[32,256]{1,0:T(8,128)} reduce(f32[4,32,256]{2,1,0:T(8,128)S(1)} %all_to_all.5, f32[]{:T(128)} %constant.0.clone.1), dimensions={0}, to_apply=%region_0.0 | reduce | flops 24576 | bytes 163844 | tf_op jit(solution)/shard_map/reduce_sum | solution.py:185

commit v3 on v2

--- a/solution.py
+++ b/solution.py
@@ -11,10 +11,11 @@
 DIFFUSIVITY = 1.66
 LOG2E = 1.0 / math.log(2.0)
 SUBLANES = 8
-
-
-def gelu(values):
-    return 0.5 * values * (1.0 + lax.erf(values * math.sqrt(0.5)))
+SHIFTED = 3
+
+
+def twice_gelu(values):
+    return values * (1.0 + lax.erf(values * math.sqrt(0.5)))
 
 
 def group_sum(values):
@@ -29,26 +30,26 @@
         refs[25:],
     )
     copies = [pltpu.make_async_copy(a, b, sems.at[i]) for i, (a, b) in enumerate(zip(hbm, local))]
-    for copy in copies[:10]:
+    for copy in copies[:7]:
         copy.start()
     (
+        absorption_ref,
         state_ref,
+        zenith_ref,
+        scatter_ref,
+        solar_ref,
         sunlit_ref,
+        albedo_ref,
         flagged_ref,
-        zenith_ref,
-        albedo_ref,
         bias_one_ref,
         bias_two_ref,
-        absorption_ref,
-        scatter_ref,
-        solar_ref,
         weight_one_ref,
         weight_two_ref,
     ) = local
-    for copy in copies[:10]:
+    for copy in copies[7:]:
+        copy.start()
+    for copy in copies[:7]:
         copy.wait()
-    for copy in copies[10:]:
-        copy.start()
 
     groups, levels = absorption_ref.shape
     columns = state_ref.shape[0]
@@ -60,7 +61,6 @@
         return pl.ds(level * chains, chains)
 
     lit = sunlit_ref[...].astype(jnp.float32)
-    chosen = flagged_ref[...].astype(jnp.float32)
     zenith = zenith_ref[...].astype(jnp.float32)
     albedo = albedo_ref[...].astype(jnp.float32)
 
@@ -70,10 +70,10 @@
     humid_slant[...] = humidity * (1.0 / (DIFFUSIVITY * zenith))
     scaled = absorption_ref[...] * (-DIFFUSIVITY * LOG2E)
 
-    half_omega = jnp.broadcast_to(0.5 * scatter_ref[...], (levels, groups)).T
-    half_omega = jnp.broadcast_to(half_omega[:, :1], (groups, columns)).reshape(wide)
-    solar = jnp.broadcast_to(solar_ref[...], (levels, groups)).T
-    solar = jnp.broadcast_to(solar[:, :1], (groups, columns)).reshape(wide)
+    first_row = lax.broadcasted_iota(jnp.int32, (SUBLANES, groups), 0) == 0
+    sides = jnp.where(first_row, 0.5 * scatter_ref[...], solar_ref[...]).T
+    half_omega = jnp.broadcast_to(sides[:, :1], (groups, columns)).reshape(wide)
+    solar = jnp.broadcast_to(sides[:, 1:2], (groups, columns)).reshape(wide)
 
     nothing = jnp.zeros(wide, jnp.float32)
     direct = solar * (zenith * lit)
@@ -88,7 +88,7 @@
         lost[rows(level)] = half_omega - half_omega * passed
         source[rows(level)] = first
         falling[rows(level)] = down
-        total[level] = group_sum(direct)
+        total[level] = group_sum(direct) + group_sum(down[:SHIFTED])
         down = passed * down + first
         direct = below
 
@@ -99,7 +99,7 @@
             if not last:
                 source[rows(level)] = lost[rows(level)] * (falls + up)
             up = keep[rows(level)] * up + emitted
-            net = total[level] + group_sum(falls - up)
+            net = total[level] + group_sum(falls[SHIFTED:] - up[SHIFTED:]) - group_sum(up[:SHIFTED])
             if last:
                 humid[pl.ds(level, 1), :] = jnp.sum(net, axis=0, keepdims=True)
             else:
@@ -109,6 +109,7 @@
         down = nothing
         for level in range(levels):
             falling[rows(level)] = down
+            total[level] += group_sum(down[:SHIFTED])
             down = keep[rows(level)] * down + source[rows(level)]
         return down
 
@@ -117,16 +118,17 @@
         return albedo * ascend()
 
     up = lax.fori_loop(0, SWEEPS, sweep, albedo * (direct + down))
-    for copy in copies[10:]:
+    for copy in copies[7:]:
         copy.wait()
     descend(up, True)
 
+    chosen = flagged_ref[...].astype(jnp.float32)
     exact = (humid[...] * chosen).T
 
     hidden = jnp.dot(state_ref[...], weight_one_ref[...], preferred_element_type=jnp.float32)
-    hidden = gelu(hidden + bias_one_ref[...].astype(jnp.float32)).astype(jnp.bfloat16)
+    hidden = twice_gelu(hidden + bias_one_ref[...].astype(jnp.float32)).astype(jnp.bfloat16)
     guess = jnp.dot(hidden, weight_two_ref[...], preferred_element_type=jnp.float32)
-    guess = 0.25 * (guess + bias_two_ref[...].astype(jnp.float32))
+    guess = 0.125 * guess + 0.25 * bias_two_ref[...].astype(jnp.float32)
     mask = jnp.broadcast_to((1.0 - chosen) * lit, (levels, columns)).T
     out_ref[:, :levels] = exact + mask * guess[:, :levels]
     out_ref[:, levels:] = guess[:, levels:]
@@ -152,16 +154,16 @@
     outputs = second_weight.shape[2]
     bands = lax.axis_size("band")
     operands = (
+        absorption,
         column_state,
+        cos_zenith.reshape(1, columns),
+        scatter_albedo.reshape(1, groups),
+        solar_weight.reshape(1, groups),
         sunlit.reshape(1, columns),
+        surface_albedo.reshape(1, columns),
         flagged.reshape(1, columns),
-        cos_zenith.reshape(1, columns),
-        surface_albedo.reshape(1, columns),
         first_bias,
         second_bias,
-        absorption,
-        scatter_albedo.reshape(1, groups),
-        solar_weight.reshape(1, groups),
         first_weight[0],
         second_weight[0],
     )
@@ -173,7 +175,7 @@
         out_specs=pl.BlockSpec(memory_space=pltpu.VMEM),
         scratch_shapes=[pltpu.VMEM(x.shape, x.dtype) for x in operands]
         + [pltpu.VMEM((levels, columns), jnp.float32)] * 2
-        + [pltpu.VMEM((chain_rows, SUBLANES, columns), jnp.float32)] * 4
+        + [pltpu.VMEM((chain_rows + SUBLANES, SUBLANES, columns), jnp.float32)] * 4
         + [pltpu.VMEM((levels, SUBLANES, columns), jnp.float32)]
         + [pltpu.SemaphoreType.DMA((len(operands),))],
         compiler_params=pltpu.CompilerParams(vmem_limit_bytes=48 * 1024 * 1024),

time: 21.8 us -> 21.7 us (level)
  no operation moved by 1% of the time
where the time goes in v3:
time: 21.7 us; the launch traced here: 21.5 us
  blocking collectives  12.7 us (59%)
  Pallas kernels  8.18 us (38%)
  other arithmetic  0.62 us (3%)
    all_to_all x1, blocking collectives, shards(): lax.all_to_all(terms.reshape(bands, columns // bands, outputs), 'band', s...  12.7 us
    pallas_call x1, Pallas kernels, shards(): pl.pallas_call(column_kernel, out_shape=jax.ShapeDtypeStruct((columns, ou...  8.18 us
    reduce_sum x1, other arithmetic, shards(): return jnp.sum(blocks, axis=0)  0.62 us

profile of v3, /device:TPU:8, one launch (start us, length us, event | category | flops | bytes accessed | tf_op | source)
XLA Modules:
  0.0 21.5 jit_solution(10073953795936392541)
XLA Ops:
  0.0 8.2 %column_terms.1 = f32[128,256]{1,0:T(8,128)S(1)} custom-call(f32[56,128]{1,0:T(8,128)} %refs_0_.1, bf16[128,512]{1,0:T(8,128)(2,1)} %refs_1_.1, bf16[1,128]{1,0:T(2,128)(2,1)} %bitcast.12, f32[1,56]{1,0:T(1,128)} %bitcast.13, f32[1,56]{1,0:T(1,128)} %bitcast.14, s32[1,128]{1,0:T(1,128)} %bitcast.15, bf16[1,128]{1,0:T(2,128)(2,1)} %bitcast.16, ...), custom_call_target="tpu_custom_call" | custom-call | tf_op jit(solution)/shard_map/column_terms/pallas_call | solution.py:171
  8.2 12.7 %all_to_all.5 = f32[4,32,256]{2,1,0:T(8,128)S(1)} all-to-all(f32[4,32,256]{2,1,0:T(8,128)S(1)} %bitcast.9), channel_id=1, replica_groups=mesh['tile'=128,'band'=4] {'band'}, dimensions={0} | all-to-all | bytes 262144 | tf_op jit(solution)/shard_map/all_to_all | solution.py:184
  20.9 0.6 %reduce_sum.9 = f32[32,256]{1,0:T(8,128)} reduce(f32[4,32,256]{2,1,0:T(8,128)S(1)} %all_to_all.5, f32[]{:T(128)} %constant.0.clone.1), dimensions={0}, to_apply=%region_0.0 | reduce | flops 24576 | bytes 163844 | tf_op jit(solution)/shard_map/reduce_sum | solution.py:187
